TPU v7x, 256 devices: a whole 4x4x8 slice. The times are simulated.
256 devices in a mesh: dp: 32 (over z_lo, x, core), rows: 8 (over z_hi, y).
Axes of the slice: x: 4, y: 4, z: 8 (z_hi: 2, z_lo: 4; z = z_hi * 4 + z_lo), core: 2. Of those that a mesh axis runs over, the one named last changes fastest.
Arguments:
- features: bfloat16 [64, 48, 64, 1024], P('dp', 'rows'), may hold values from -8 to 8
- first_atrous_weight: bfloat16 [3, 3, 1024, 256], P(None, None, 'dp'), may hold values from -0.0625 to 0.0625
- second_atrous_weight: bfloat16 [3, 3, 1024, 256], P(None, None, 'dp'), may hold values from -0.0625 to 0.0625
- third_atrous_weight: bfloat16 [3, 3, 1024, 256], P(None, None, 'dp'), may hold values from -0.0625 to 0.0625
- pointwise_weight: bfloat16 [1024, 256], replicated, may hold values from -0.1875 to 0.1875
- pooling_weight: bfloat16 [1024, 256], replicated, may hold values from -0.1875 to 0.1875
- projection_weight: bfloat16 [1280, 256], replicated, may hold values from -0.15625 to 0.15625
- branch_norm_gain: float32 [4, 256], replicated, may hold values from 0.25 to 1.75
- branch_norm_shift: float32 [4, 256], replicated, may hold values from -3 to 3
- projection_norm_gain: float32 [256], replicated, may hold values from 0.25 to 1.75
- projection_norm_shift: float32 [256], replicated, may hold values from -3 to 3
- ghost_group_index: int32 [64], replicated, may hold values from 0 to 15, as said below
Outputs:
- decoder_in: bfloat16 [64, 48, 64, 256], P(None, 'rows', 'dp')
Inputs may be any that keep to these rules, and one draw needn't show every extreme that they name: `ghost_group_index`: each of the 16 group ids names exactly 4 images.
All inputs are finite; a program needn't handle non-finite values.
Results may differ from a plain program's by a relative error of at most 0.0014.
The roundings to bfloat16 on the way count: a program that leaves them out, or rounds other values in their place, can miss the bound.
Values may be sent and summed in bfloat16 or wider, within the bound.
A program may use at most 128 MiB of HBM per device.

v0:
```python
import jax
import jax.numpy as jnp
from jax import lax
from jax.sharding import PartitionSpec as P

DILATION_FIRST = 12
DILATION_SECOND = 24
DILATION_THIRD = 36


def from_behind(array, axis, by):
    count = lax.axis_size(axis)
    pairs = [(i, i + by) for i in range(count) if 0 <= i + by < count]
    return lax.ppermute(array, axis, pairs)


def row_tap_list(block_tensor, kernel_row_slice, dilation_rate):
    partial_terms = jnp.einsum(
        "irwc,kco->irwko", block_tensor, kernel_row_slice, preferred_element_type=jnp.float32
    )
    map_width = block_tensor.shape[2]
    left_padding = jnp.pad(partial_terms[:, :, :, 0], ((0, 0), (0, 0), (dilation_rate, 0), (0, 0)))[
        :, :, :map_width
    ]
    right_padding = jnp.pad(
        partial_terms[:, :, :, 2], ((0, 0), (0, 0), (0, dilation_rate), (0, 0))
    )[:, :, dilation_rate:]
    return partial_terms[:, :, :, 1] + left_padding + right_padding


def dilated_result(features, kernel_weight, dilation_rate):
    step_offsets = dilation_rate // features.shape[1]
    running_sum = row_tap_list(features, kernel_weight[1], dilation_rate)
    for by_dev, tap_offset in ((step_offsets, 0), (-step_offsets, 2)):
        shifted_rows = from_behind(features, "rows", by_dev)
        running_sum = running_sum + row_tap_list(
            shifted_rows, kernel_weight[tap_offset], dilation_rate
        )
    return running_sum


def stats_terms(pre, onehot):
    first = jnp.sum(pre, axis=(1, 2))
    second = jnp.sum(pre * pre, axis=(1, 2))
    group_first = jnp.dot(onehot.T, first, precision=lax.Precision.HIGHEST)
    group_second = jnp.dot(onehot.T, second, precision=lax.Precision.HIGHEST)
    return (group_first, group_second)


def apply_norm(pre, onehot, total_first, total_second, count, gain, shift):
    mean = total_first / count
    var = total_second / count - mean * mean
    inv = lax.rsqrt(var + 1e-05)
    img_mean = jnp.dot(onehot, mean, precision=lax.Precision.HIGHEST)
    img_inv = jnp.dot(onehot, inv, precision=lax.Precision.HIGHEST)
    scaled = (pre - img_mean[:, None, None, :]) * img_inv[:, None, None, :] * gain + shift
    return jax.nn.relu(scaled).astype(jnp.bfloat16)


def project(joined, onehot, projection_weight, count, projection_norm_gain, projection_norm_shift):
    proj = jnp.einsum(
        "irwc,co->irwo", joined, projection_weight, preferred_element_type=jnp.float32
    )
    group_first, group_second = stats_terms(proj, onehot)
    total_first, total_second = lax.psum((group_first, group_second), ("dp", "rows"))
    return apply_norm(
        proj, onehot, total_first, total_second, count, projection_norm_gain, projection_norm_shift
    )


def shards(
    features,
    first_atrous_weight,
    second_atrous_weight,
    third_atrous_weight,
    pointwise_weight,
    pooling_weight,
    projection_weight,
    branch_norm_gain,
    branch_norm_shift,
    projection_norm_gain,
    projection_norm_shift,
    ghost_group_index,
):
    img_dev, rows_dev, cols, chans = features.shape
    dp_size = lax.axis_size("dp")
    rows_size = lax.axis_size("rows")
    images = img_dev * dp_size
    groups = images // 4
    pixels = rows_dev * rows_size * cols
    count = 4.0 * pixels
    start = lax.axis_index("dp") * img_dev
    labels = jnp.arange(groups, dtype=jnp.int32)
    all_hot = (ghost_group_index[:, None] == labels[None, :]).astype(jnp.float32)
    own_hot = lax.dynamic_slice_in_dim(all_hot, start, img_dev, 0)
    first_kernel, second_kernel, third_kernel = (
        lax.all_gather(first_atrous_weight, "dp", axis=2, tiled=True),
        lax.all_gather(second_atrous_weight, "dp", axis=2, tiled=True),
        lax.all_gather(third_atrous_weight, "dp", axis=2, tiled=True),
    )
    pointwise_output = jnp.einsum(
        "irwc,co->irwo", features, pointwise_weight, preferred_element_type=jnp.float32
    )
    pre = jnp.concatenate(
        [
            pointwise_output,
            dilated_result(features, first_kernel, DILATION_FIRST),
            dilated_result(features, second_kernel, DILATION_SECOND),
            dilated_result(features, third_kernel, DILATION_THIRD),
        ],
        -1,
    )
    group_first, group_second = stats_terms(pre, own_hot)
    pool_part = jnp.sum(features, axis=(1, 2), dtype=jnp.float32)
    pool_total = lax.psum(pool_part, "rows")
    total_first, total_second = lax.psum((group_first, group_second), ("dp", "rows"))
    branches = apply_norm(
        pre,
        own_hot,
        total_first,
        total_second,
        count,
        branch_norm_gain.reshape(-1),
        branch_norm_shift.reshape(-1),
    )
    pooled = (pool_total / pixels).astype(jnp.bfloat16)
    pool_act = jax.nn.relu(
        jnp.dot(pooled, pooling_weight, preferred_element_type=jnp.float32)
    ).astype(jnp.bfloat16)
    pool_map = jnp.broadcast_to(
        pool_act[:, None, None, :], (img_dev, rows_dev, cols, pool_act.shape[1])
    )
    joined = jnp.concatenate([branches, pool_map], -1)
    local_out = project(
        joined, own_hot, projection_weight, count, projection_norm_gain, projection_norm_shift
    )
    return lax.all_to_all(local_out, "dp", split_axis=2, concat_axis=0, tiled=True)


def solution(mesh):
    in_specs = (
        P("dp", "rows", None, None),
        P(None, None, "dp", None),
        P(None, None, "dp", None),
        P(None, None, "dp", None),
        P(),
        P(),
        P(),
        P(),
        P(),
        P(),
        P(),
        P(),
    )
    out_specs = P(None, "rows", "dp", None)
    return jax.shard_map(shards, mesh=mesh, in_specs=in_specs, out_specs=out_specs, check_vma=False)
```

profile of v0, /device:TPU:1, one launch (start us, length us, event | category | flops | bytes accessed | tf_op | source)
XLA Modules:
  0.0 726.8 jit_solution(7017526560821502395)
XLA Ops:
  10.1 7.5 %collective-permute-start = (bf16[2,6,64,1024]{3,2,1,0:T(8,128)(2,1)}, bf16[2,6,64,1024]{3,2,1,0:T(8,128)(2,1)}, u32[]{:S(2)}, u32[]{:S(2)}) collective-permute-start(bf16[2,6,64,1024]{3,2,1,0:T(8,128)(2,1)} %param.12), channel_id=1, source_target_pairs={{0,2},{1,3},{2,4},{3,5},{4,6},{5,7},{8,10},{9,11},{10,12},{11,13},... | collective-permute-start | bytes 4718600 | tf_op jit(solution)/shard_map/ppermute | solution.py:14
  18.9 11.2 %collective-permute-start.2 = (bf16[2,6,64,1024]{3,2,1,0:T(8,128)(2,1)}, bf16[2,6,64,1024]{3,2,1,0:T(8,128)(2,1)}, u32[]{:S(2)}, u32[]{:S(2)}) collective-permute-start(bf16[2,6,64,1024]{3,2,1,0:T(8,128)(2,1)} %param.12), channel_id=1, source_target_pairs={{0,4},{1,5},{2,6},{3,7},{8,12},{9,13},{10,14},{11,15},{16,20},{17,... | collective-permute-start | bytes 4718600 | tf_op jit(solution)/shard_map/ppermute | solution.py:14
  32.1 1.7 convert_reduce_fusion
  33.9 146.7 %psum.37 = f32[2,1024]{1,0:T(2,128)S(1)} all-reduce(f32[2,1024]{1,0:T(2,128)S(1)} %convert_reduce_fusion), channel_id=1, replica_groups=mesh['dp'=32,'rows'=8] {'rows'}, use_global_device_ids=true, to_apply=%region_5.6 | all-reduce | flops 2048 | bytes 16384 | tf_op jit(solution)/shard_map/psum | solution.py:115
  180.5 2.1 fusion.49
  182.7 2.4 collective-permute-start.4
  185.1 3.4 fusion.10
  189.9 2.8 fusion.11
  197.4 90.0 %all-gather.6.cloned.1.call-done = bf16[3,3,1024,256]{3,2,1,0:T(8,128)(2,1)} async-done(((bf16[3,3,32,256]{3,2,1,0:T(8,128)(2,1)}), bf16[3,3,1024,256]{3,2,1,0:T(8,128)(2,1)}) %all-gather.6.cloned.1.call-update) | async-done | bytes 4718608 | tf_op jit(solution)/shard_map/all_gather | solution.py:98
  287.4 3.4 fusion.7
  290.8 1.4 slice_bitcast_fusion.27
  292.3 2.8 fusion.8
  295.1 1.4 slice_bitcast_fusion.30
  297.9 1.5 slice_bitcast_fusion.33
  299.8 61.1 %all-gather.8.cloned.1.call-done = bf16[3,3,1024,256]{3,2,1,0:T(8,128)(2,1)} async-done(((bf16[3,3,32,256]{3,2,1,0:T(8,128)(2,1)}), bf16[3,3,1024,256]{3,2,1,0:T(8,128)(2,1)}) %all-gather.8.cloned.1.call-update) | async-done | bytes 4718608 | tf_op jit(solution)/shard_map/all_gather | solution.py:99
  361.0 3.4 fusion.4
  364.5 2.8 fusion.5
  367.5 1.4 fusion.6
  370.8 2.3 fusion.26
  373.8 1.9 fusion.34
  381.0 237.9 %all-reduce.22.cloned.1.call-done = (f32[16,1024]{1,0:T(8,128)}, f32[16,1024]{1,0:T(8,128)}) async-done(((f32[16,1024]{1,0:T(8,128)}, f32[16,1024]{1,0:T(8,128)}), (f32[16,1024]{1,0:T(8,128)}, f32[16,1024]{1,0:T(8,128)})) %all-reduce.22.cloned.1.call-update) | async-done | bytes 131088 | tf_op jit(solution)/shard_map/psum | solution.py:116
  621.0 1.7 maximum_convert_fusion
  624.1 76.6 %all-reduce.18 = (f32[16,256]{1,0:T(8,128)S(1)}, f32[16,256]{1,0:T(8,128)S(1)}) all-reduce(f32[16,256]{1,0:T(8,128)S(1)} %fusion.76, f32[16,256]{1,0:T(8,128)S(1)} %fusion.77), channel_id=1, replica_groups=mesh['dp'=32,'rows'=8] {'dp','rows'}, use_global_device_ids=true, to_apply=%region_9.10 | all-reduce | flops 8192 | bytes 65536 | tf_op jit(solution)/shard_map/psum | solution.py:65
  701.6 17.6 %all_to_all.18 = bf16[2,6,64,256]{3,0,1,2:T(2,128)(2,1)S(1)} all-to-all(bf16[2,6,64,256]{3,0,1,2:T(2,128)(2,1)S(1)} %copy.97), channel_id=1, replica_groups=mesh['dp'=32,'rows'=8] {'dp'}, dimensions={2} | all-to-all | bytes 786432 | tf_op jit(solution)/shard_map/all_to_all | solution.py:137
  (99 shorter events, 28.2 us)
Async XLA Ops:
  6.5 616.3 %copy-start = (bf16[1280,256]{1,0:T(8,128)(2,1)S(1)}, bf16[1280,256]{1,0:T(8,128)(2,1)}, u32[]{:S(2)}) copy-start(bf16[1280,256]{1,0:T(8,128)(2,1)} %param.18) | copy-start | bytes 1966084
  6.5 178.6 %all-gather.4.cloned.1.call-start = ((), (), s32[]{:S(2)}) async-start(), calls=%async_computation.1 | async-start | bytes 4866048 | tf_op jit(solution)/shard_map/all_gather | solution.py:97
  7.3 280.2 %all-gather.6.cloned.1.call-start = ((), (), s32[]{:S(2)}) async-start(), calls=%async_computation.2 | async-start | bytes 4866048 | tf_op jit(solution)/shard_map/all_gather | solution.py:98
  8.0 174.6 %copy-start.2 = (bf16[2,6,64,1024]{3,2,1,0:T(8,128)(2,1)S(1)}, bf16[2,6,64,1024]{3,2,1,0:T(8,128)(2,1)}, u32[]{:S(2)}) copy-start(bf16[2,6,64,1024]{3,2,1,0:T(8,128)(2,1)} %param.12) | copy-start | bytes 4718596
  8.0 352.9 %all-gather.8.cloned.1.call-start = ((), (), s32[]{:S(2)}) async-start(), calls=%async_computation.3 | async-start | bytes 4866048 | tf_op jit(solution)/shard_map/all_gather | solution.py:99
  8.8 610.2 %all-reduce.22.cloned.1.call-start = ((), (), s32[]{:S(2)}) async-start(), calls=%async_computation.4 | async-start | bytes 262144 | tf_op jit(solution)/shard_map/psum | solution.py:116
  8.8 173.8 %collective-permute-start.1 = (bf16[2,6,64,1024]{3,2,1,0:T(8,128)(2,1)}, bf16[2,6,64,1024]{3,2,1,0:T(8,128)(2,1)}, u32[]{:S(2)}, u32[]{:S(2)}) collective-permute-start(bf16[2,6,64,1024]{3,2,1,0:T(8,128)(2,1)} %param.12), channel_id=1, source_target_pairs={{2,0},{3,1},{4,2},{5,3},{6,4},{7,5},{10,8},{11,9},{12,10},{13,11},... | collective-permute-start | bytes 4718600 | tf_op jit(solution)/shard_map/ppermute | solution.py:14
  10.1 179.8 %collective-permute-start = (bf16[2,6,64,1024]{3,2,1,0:T(8,128)(2,1)}, bf16[2,6,64,1024]{3,2,1,0:T(8,128)(2,1)}, u32[]{:S(2)}, u32[]{:S(2)}) collective-permute-start(bf16[2,6,64,1024]{3,2,1,0:T(8,128)(2,1)} %param.12), channel_id=1, source_target_pairs={{0,2},{1,3},{2,4},{3,5},{4,6},{5,7},{8,10},{9,11},{10,12},{11,13},... | collective-permute-start | bytes 4718600 | tf_op jit(solution)/shard_map/ppermute | solution.py:14
  17.6 179.9 %collective-permute-start.3 = (bf16[2,6,64,1024]{3,2,1,0:T(8,128)(2,1)}, bf16[2,6,64,1024]{3,2,1,0:T(8,128)(2,1)}, u32[]{:S(2)}, u32[]{:S(2)}) collective-permute-start(bf16[2,6,64,1024]{3,2,1,0:T(8,128)(2,1)} %param.12), channel_id=1, source_target_pairs={{4,0},{5,1},{6,2},{7,3},{12,8},{13,9},{14,10},{15,11},{20,16},{21,... | collective-permute-start | bytes 4718600 | tf_op jit(solution)/shard_map/ppermute | solution.py:14
  18.9 273.4 %collective-permute-start.2 = (bf16[2,6,64,1024]{3,2,1,0:T(8,128)(2,1)}, bf16[2,6,64,1024]{3,2,1,0:T(8,128)(2,1)}, u32[]{:S(2)}, u32[]{:S(2)}) collective-permute-start(bf16[2,6,64,1024]{3,2,1,0:T(8,128)(2,1)} %param.12), channel_id=1, source_target_pairs={{0,4},{1,5},{2,6},{3,7},{8,12},{9,13},{10,14},{11,15},{16,20},{17,... | collective-permute-start | bytes 4718600 | tf_op jit(solution)/shard_map/ppermute | solution.py:14
  30.1 269.7 %collective-permute-start.5 = (bf16[2,6,64,1024]{3,2,1,0:T(8,128)(2,1)}, bf16[2,6,64,1024]{3,2,1,0:T(8,128)(2,1)}, u32[]{:S(2)}, u32[]{:S(2)}) collective-permute-start(bf16[2,6,64,1024]{3,2,1,0:T(8,128)(2,1)} %param.12), channel_id=1, source_target_pairs={{6,0},{7,1},{14,8},{15,9},{22,16},{23,17},{30,24},{31,25},{38,32},... | collective-permute-start | bytes 4718600 | tf_op jit(solution)/shard_map/ppermute | solution.py:14
  182.7 181.9 %collective-permute-start.4 = (bf16[2,6,64,1024]{3,2,1,0:T(8,128)(2,1)S(1)}, bf16[2,6,64,1024]{3,2,1,0:T(8,128)(2,1)}, u32[]{:S(2)}, u32[]{:S(2)}) collective-permute-start(bf16[2,6,64,1024]{3,2,1,0:T(8,128)(2,1)S(1)} %copy-done.2), channel_id=1, source_target_pairs={{0,6},{1,7},{8,14},{9,15},{16,22},{17,23},{24,30},{25,31},{32,38},... | collective-permute-start | bytes 4718600 | tf_op jit(solution)/shard_map/ppermute | solution.py:14
  185.1 4.8 copy-start.26
  188.5 4.2 copy-start.15
  192.7 2.8 copy-start.16
  287.4 4.8 copy-start.25
  290.8 4.2 copy-start.18
  295.1 2.8 copy-start.19
  361.0 3.6 copy-start.24
  370.8 2.5 copy-start.12
  370.8 2.8 copy-start.13
  370.8 3.0 copy-start.14
  622.8 78.2 %copy-start.22 = (f32[256]{0:T(256)S(1)}, f32[256]{0:T(256)}, u32[]{:S(2)}) copy-start(f32[256]{0:T(256)} %param.22) | copy-start | bytes 3076
  622.8 78.2 %copy-start.23 = (f32[256]{0:T(256)S(1)}, f32[256]{0:T(256)}, u32[]{:S(2)}) copy-start(f32[256]{0:T(256)} %param.21) | copy-start | bytes 3076
  (13 other events, 23.1 us)
Sparse Core Ops, SparseCore 0:
  9.2 144.8 all-gather.3
  156.0 131.4 all-gather.5
  289.3 71.6 all-gather.7
  379.6 239.3 all-reduce.21
where the time goes:
time: 728 us; the launch traced here: 727 us
  waiting for transfers between devices  391 us (54%)
  blocking collectives  241 us (33%)
  matrix products  30.6 us (4%)
  starting transfers between devices  25.1 us (3%)
  local copies, waits for them, and re-layouts  16.8 us (2%)
  between operations  13.6 us (2%)
  other arithmetic  8.76 us (1%)
    psum x1, waiting for transfers between devices, shards(): lax.psum((group_first, group_second), ('dp', 'rows'))  238 us
    psum x1, blocking collectives, shards(): pool_total = lax.psum(pool_part, 'rows')  147 us
    all_gather x1, waiting for transfers between devices, shards(): lax.all_gather(second_atrous_weight, 'dp', axis=2, tiled=True)  90 us
    psum x1, blocking collectives, project(): lax.psum((group_first, group_second), ('dp', 'rows'))  76.6 us
    all_gather x1, waiting for transfers between devices, shards(): lax.all_gather(third_atrous_weight, 'dp', axis=2, tiled=True)  61.1 us
    ppermute x6, starting transfers between devices, from_behind(): return lax.ppermute(array, axis, pairs)  25 us
    dot_general x9, matrix products, row_tap_list(): jnp.einsum('irwc,kco->irwko', block_tensor, kernel_row_slice, preferred_e...  22.8 us
    all_to_all x1, blocking collectives, shards(): lax.all_to_all(local_out, 'dp', split_axis=2, concat_axis=0, tiled=True)  17.6 us
  transfers between devices with their start and end apart: 10, of which 3 were waited for; matrix products, arithmetic and copies ran while one was open for 5% of the time, Pallas kernels for 0%

commit v1 on v0

--- a/solution.py
+++ b/solution.py
@@ -112,7 +112,8 @@
     )
     group_first, group_second = stats_terms(pre, own_hot)
     pool_part = jnp.sum(features, axis=(1, 2), dtype=jnp.float32)
-    pool_total = lax.psum(pool_part, "rows")
+    built = lax.all_gather(pool_part, "rows")
+    pool_total = jnp.sum(built, 0)
     total_first, total_second = lax.psum((group_first, group_second), ("dp", "rows"))
     branches = apply_norm(
         pre,

time: 728 us -> 743 us (1.021)
  waiting for transfers between devices: 391 us -> 400 us
    all_gather x0 -> x1, blocking collectives: none -> 152 us  [shards(): built = lax.all_gather(pool_part, 'rows')]
    psum x1 -> x0, blocking collectives: 147 us -> none  [shards(): pool_total = lax.psum(pool_part, 'rows')]
  transfers between devices with their start and end apart: 10 -> 10, of which waited for: 3 -> 3; matrix products, arithmetic and copies ran while one was open for 5% -> 4% of each run, Pallas kernels for 0% -> 0%
where the time goes in v1:
time: 743 us; the launch traced here: 742 us
  waiting for transfers between devices  400 us (54%)
  blocking collectives  247 us (33%)
  matrix products  29 us (4%)
  starting transfers between devices  27 us (4%)
  local copies, waits for them, and re-layouts  16.8 us (2%)
  between operations  13.6 us (2%)
  other arithmetic  8.83 us (1%)
    psum x1, waiting for transfers between devices, shards(): lax.psum((group_first, group_second), ('dp', 'rows'))  238 us
    all_gather x1, blocking collectives, shards(): built = lax.all_gather(pool_part, 'rows')  152 us
    all_gather x1, waiting for transfers between devices, shards(): lax.all_gather(second_atrous_weight, 'dp', axis=2, tiled=True)  94.9 us
    psum x1, blocking collectives, project(): lax.psum((group_first, group_second), ('dp', 'rows'))  76.6 us
    all_gather x1, waiting for transfers between devices, shards(): lax.all_gather(third_atrous_weight, 'dp', axis=2, tiled=True)  65.3 us
    ppermute x6, starting transfers between devices, from_behind(): return lax.ppermute(array, axis, pairs)  26.8 us
    dot_general x9, matrix products, row_tap_list(): jnp.einsum('irwc,kco->irwko', block_tensor, kernel_row_slice, preferred_e...  22.7 us
    all_to_all x1, blocking collectives, shards(): lax.all_to_all(local_out, 'dp', split_axis=2, concat_axis=0, tiled=True)  17.6 us
  transfers between devices with their start and end apart: 10, of which 3 were waited for; matrix products, arithmetic and copies ran while one was open for 4% of the time, Pallas kernels for 0%

profile of v1, /device:TPU:1, one launch (start us, length us, event | category | flops | bytes accessed | tf_op | source)
XLA Modules:
  0.0 742.1 jit_solution(6463600554907869608)
XLA Ops:
  10.1 7.5 %collective-permute-start = (bf16[2,6,64,1024]{3,2,1,0:T(8,128)(2,1)}, bf16[2,6,64,1024]{3,2,1,0:T(8,128)(2,1)}, u32[]{:S(2)}, u32[]{:S(2)}) collective-permute-start(bf16[2,6,64,1024]{3,2,1,0:T(8,128)(2,1)} %param.12), channel_id=1, source_target_pairs={{0,2},{1,3},{2,4},{3,5},{4,6},{5,7},{8,10},{9,11},{10,12},{11,13},... | collective-permute-start | bytes 4718600 | tf_op jit(solution)/shard_map/ppermute | solution.py:14
  18.8 11.3 %collective-permute-start.2 = (bf16[2,6,64,1024]{3,2,1,0:T(8,128)(2,1)}, bf16[2,6,64,1024]{3,2,1,0:T(8,128)(2,1)}, u32[]{:S(2)}, u32[]{:S(2)}) collective-permute-start(bf16[2,6,64,1024]{3,2,1,0:T(8,128)(2,1)} %param.12), channel_id=1, source_target_pairs={{0,4},{1,5},{2,6},{3,7},{8,12},{9,13},{10,14},{11,15},{16,20},{17,... | collective-permute-start | bytes 4718600 | tf_op jit(solution)/shard_map/ppermute | solution.py:14
  32.2 1.7 convert_reduce_fusion
  33.9 152.4 %all-gather.1 = f32[8,2,1024]{2,1,0:T(2,128)S(1)} all-gather(f32[1,2,1024]{2,1,0:T(2,128)S(1)} %bitcast.188), channel_id=2, replica_groups=mesh['dp'=32,'rows'=8] {'rows'}, dimensions={0}, use_global_device_ids=true | all-gather | bytes 73728 | tf_op jit(solution)/shard_map/all_gather | solution.py:115
  187.0 4.2 collective-permute-start.4
  191.2 3.4 fusion.10
  196.0 2.8 fusion.11
  203.5 94.9 %all-gather.8.cloned.1.call-done = bf16[3,3,1024,256]{3,2,1,0:T(8,128)(2,1)} async-done(((bf16[3,3,32,256]{3,2,1,0:T(8,128)(2,1)}), bf16[3,3,1024,256]{3,2,1,0:T(8,128)(2,1)}) %all-gather.8.cloned.1.call-update) | async-done | bytes 4718608 | tf_op jit(solution)/shard_map/all_gather | solution.py:98
  298.5 3.4 fusion.7
  301.9 1.4 slice_bitcast_fusion.27
  303.3 2.8 fusion.8
  306.2 1.4 slice_bitcast_fusion.30
  307.6 1.4 fusion.9
  309.0 1.5 slice_bitcast_fusion.33
  310.9 65.3 %all-gather.10.cloned.1.call-done = bf16[3,3,1024,256]{3,2,1,0:T(8,128)(2,1)} async-done(((bf16[3,3,32,256]{3,2,1,0:T(8,128)(2,1)}), bf16[3,3,1024,256]{3,2,1,0:T(8,128)(2,1)}) %all-gather.10.cloned.1.call-update) | async-done | bytes 4718608 | tf_op jit(solution)/shard_map/all_gather | solution.py:99
  376.3 3.4 fusion.4
  379.9 2.8 fusion.5
  382.8 1.4 fusion.6
  386.1 2.3 fusion.26
  389.1 1.9 fusion.34
  396.3 237.9 %all-reduce.22.cloned.1.call-done = (f32[16,1024]{1,0:T(8,128)}, f32[16,1024]{1,0:T(8,128)}) async-done(((f32[16,1024]{1,0:T(8,128)}, f32[16,1024]{1,0:T(8,128)}), (f32[16,1024]{1,0:T(8,128)}, f32[16,1024]{1,0:T(8,128)})) %all-reduce.22.cloned.1.call-update) | async-done | bytes 131088 | tf_op jit(solution)/shard_map/psum | solution.py:117
  636.4 1.7 maximum_convert_fusion
  639.4 76.6 %all-reduce.18 = (f32[16,256]{1,0:T(8,128)S(1)}, f32[16,256]{1,0:T(8,128)S(1)}) all-reduce(f32[16,256]{1,0:T(8,128)S(1)} %fusion.76, f32[16,256]{1,0:T(8,128)S(1)} %fusion.77), channel_id=1, replica_groups=mesh['dp'=32,'rows'=8] {'dp','rows'}, use_global_device_ids=true, to_apply=%region_9.10 | all-reduce | flops 8192 | bytes 65536 | tf_op jit(solution)/shard_map/psum | solution.py:65
  716.9 17.6 %all_to_all.18 = bf16[2,6,64,256]{3,0,1,2:T(2,128)(2,1)S(1)} all-to-all(bf16[2,6,64,256]{3,0,1,2:T(2,128)(2,1)S(1)} %copy.97), channel_id=1, replica_groups=mesh['dp'=32,'rows'=8] {'dp'}, dimensions={2} | all-to-all | bytes 786432 | tf_op jit(solution)/shard_map/all_to_all | solution.py:138
  (102 shorter events, 27.4 us)
Async XLA Ops:
  6.5 631.6 %copy-start = (bf16[1280,256]{1,0:T(8,128)(2,1)S(1)}, bf16[1280,256]{1,0:T(8,128)(2,1)}, u32[]{:S(2)}) copy-start(bf16[1280,256]{1,0:T(8,128)(2,1)} %param.18) | copy-start | bytes 1966084
  6.5 179.8 %copy-start.2 = (bf16[2,6,64,1024]{3,2,1,0:T(8,128)(2,1)S(1)}, bf16[2,6,64,1024]{3,2,1,0:T(8,128)(2,1)}, u32[]{:S(2)}) copy-start(bf16[2,6,64,1024]{3,2,1,0:T(8,128)(2,1)} %param.12) | copy-start | bytes 4718596
  6.5 179.8 %copy-start.22 = (bf16[1024,256]{1,0:T(8,128)(2,1)S(1)}, bf16[1024,256]{1,0:T(8,128)(2,1)}, u32[]{:S(2)}) copy-start(bf16[1024,256]{1,0:T(8,128)(2,1)} %param.16) | copy-start | bytes 1572868
  6.5 184.7 %all-gather.6.cloned.1.call-start = ((), (), s32[]{:S(2)}) async-start(), calls=%async_computation.1 | async-start | bytes 4866048 | tf_op jit(solution)/shard_map/all_gather | solution.py:97
  7.3 291.2 %all-gather.8.cloned.1.call-start = ((), (), s32[]{:S(2)}) async-start(), calls=%async_computation.2 | async-start | bytes 4866048 | tf_op jit(solution)/shard_map/all_gather | solution.py:98
  8.0 368.3 %all-gather.10.cloned.1.call-start = ((), (), s32[]{:S(2)}) async-start(), calls=%async_computation.3 | async-start | bytes 4866048 | tf_op jit(solution)/shard_map/all_gather | solution.py:99
  8.7 625.5 %all-reduce.22.cloned.1.call-start = ((), (), s32[]{:S(2)}) async-start(), calls=%async_computation.4 | async-start | bytes 262144 | tf_op jit(solution)/shard_map/psum | solution.py:117
  8.8 178.2 %collective-permute-start.1 = (bf16[2,6,64,1024]{3,2,1,0:T(8,128)(2,1)}, bf16[2,6,64,1024]{3,2,1,0:T(8,128)(2,1)}, u32[]{:S(2)}, u32[]{:S(2)}) collective-permute-start(bf16[2,6,64,1024]{3,2,1,0:T(8,128)(2,1)} %param.12), channel_id=1, source_target_pairs={{2,0},{3,1},{4,2},{5,3},{6,4},{7,5},{10,8},{11,9},{12,10},{13,11},... | collective-permute-start | bytes 4718600 | tf_op jit(solution)/shard_map/ppermute | solution.py:14
  10.1 185.9 %collective-permute-start = (bf16[2,6,64,1024]{3,2,1,0:T(8,128)(2,1)}, bf16[2,6,64,1024]{3,2,1,0:T(8,128)(2,1)}, u32[]{:S(2)}, u32[]{:S(2)}) collective-permute-start(bf16[2,6,64,1024]{3,2,1,0:T(8,128)(2,1)} %param.12), channel_id=1, source_target_pairs={{0,2},{1,3},{2,4},{3,5},{4,6},{5,7},{8,10},{9,11},{10,12},{11,13},... | collective-permute-start | bytes 4718600 | tf_op jit(solution)/shard_map/ppermute | solution.py:14
  17.6 186.0 %collective-permute-start.3 = (bf16[2,6,64,1024]{3,2,1,0:T(8,128)(2,1)}, bf16[2,6,64,1024]{3,2,1,0:T(8,128)(2,1)}, u32[]{:S(2)}, u32[]{:S(2)}) collective-permute-start(bf16[2,6,64,1024]{3,2,1,0:T(8,128)(2,1)} %param.12), channel_id=1, source_target_pairs={{4,0},{5,1},{6,2},{7,3},{12,8},{13,9},{14,10},{15,11},{20,16},{21,... | collective-permute-start | bytes 4718600 | tf_op jit(solution)/shard_map/ppermute | solution.py:14
  18.8 284.5 %collective-permute-start.2 = (bf16[2,6,64,1024]{3,2,1,0:T(8,128)(2,1)}, bf16[2,6,64,1024]{3,2,1,0:T(8,128)(2,1)}, u32[]{:S(2)}, u32[]{:S(2)}) collective-permute-start(bf16[2,6,64,1024]{3,2,1,0:T(8,128)(2,1)} %param.12), channel_id=1, source_target_pairs={{0,4},{1,5},{2,6},{3,7},{8,12},{9,13},{10,14},{11,15},{16,20},{17,... | collective-permute-start | bytes 4718600 | tf_op jit(solution)/shard_map/ppermute | solution.py:14
  30.1 280.8 %collective-permute-start.5 = (bf16[2,6,64,1024]{3,2,1,0:T(8,128)(2,1)}, bf16[2,6,64,1024]{3,2,1,0:T(8,128)(2,1)}, u32[]{:S(2)}, u32[]{:S(2)}) collective-permute-start(bf16[2,6,64,1024]{3,2,1,0:T(8,128)(2,1)} %param.12), channel_id=1, source_target_pairs={{6,0},{7,1},{14,8},{15,9},{22,16},{23,17},{30,24},{31,25},{38,32},... | collective-permute-start | bytes 4718600 | tf_op jit(solution)/shard_map/ppermute | solution.py:14
  187.0 192.9 %collective-permute-start.4 = (bf16[2,6,64,1024]{3,2,1,0:T(8,128)(2,1)S(1)}, bf16[2,6,64,1024]{3,2,1,0:T(8,128)(2,1)}, u32[]{:S(2)}, u32[]{:S(2)}) collective-permute-start(bf16[2,6,64,1024]{3,2,1,0:T(8,128)(2,1)S(1)} %copy-done.2), channel_id=1, source_target_pairs={{0,6},{1,7},{8,14},{9,15},{16,22},{17,23},{24,30},{25,31},{32,38},... | collective-permute-start | bytes 4718600 | tf_op jit(solution)/shard_map/ppermute | solution.py:14
  191.2 4.8 copy-start.27
  194.6 4.2 copy-start.15
  198.8 2.8 copy-start.16
  298.5 4.9 copy-start.26
  301.9 4.2 copy-start.18
  306.1 2.8 copy-start.19
  376.3 3.6 copy-start.25
  386.1 2.8 copy-start.13
  386.1 3.0 copy-start.14
  638.1 78.2 %copy-start.23 = (f32[256]{0:T(256)S(1)}, f32[256]{0:T(256)}, u32[]{:S(2)}) copy-start(f32[256]{0:T(256)} %param.22) | copy-start | bytes 3076
  638.1 78.2 %copy-start.24 = (f32[256]{0:T(256)S(1)}, f32[256]{0:T(256)}, u32[]{:S(2)}) copy-start(f32[256]{0:T(256)} %param.21) | copy-start | bytes 3076
  (14 other events, 25.7 us)
Sparse Core Ops, SparseCore 0:
  9.2 141.9 all-gather.5
  153.1 145.3 all-gather.7
  300.4 75.8 all-gather.9
  394.9 239.3 all-reduce.21
